TPU v7x, 512 devices: a whole 4x8x8 slice. The times are simulated.
512 devices in a mesh: section: 16 (over y_hi, z), ctx: 8 (over x, core), tp: 4 (over y_lo).
Axes of the slice: x: 4, y: 8 (y_hi: 2, y_lo: 4; y = y_hi * 4 + y_lo), z: 8, core: 2. Of those that a mesh axis runs over, the one named last changes fastest.
Arguments:
- queries: bfloat16 [16, 2048, 8192], P('section', 'ctx', 'tp'), may hold values from -4.5 to 4.5
- keys: bfloat16 [16, 2048, 1024], P('section', 'ctx', 'tp'), may hold values from -4.5 to 4.5
- values: bfloat16 [16, 2048, 1024], P('section', 'ctx', 'tp'), may hold values from -6 to 6
- residual: bfloat16 [16, 2048, 8192], P('section', 'ctx', 'tp'), may hold values from -1.796875 to 1.796875
- rand_blocks: int32 [16, 16, 3], P('section'), may hold values from 0 to 15, as said below
- block_order: int32 [16, 16], P('section'), may hold values from 0 to 15, each once within a row
Outputs:
- received: bfloat16 [16, 2048, 8192], P('section', 'ctx', 'tp')
Inputs may be any that keep to these rules, and one draw needn't show every extreme that they name: `rand_blocks`: query block i's entries lie in 0 to i.
All inputs are finite; a program needn't handle non-finite values.
Results may differ from a plain program's by a relative error of at most 0.0038.
Values may be sent and summed in bfloat16 or wider, within the bound.
A program may use at most 64 MiB of HBM per device.

v0:
```python
import math

import jax
import jax.numpy as jnp
from jax import lax
from jax.sharding import PartitionSpec as P

HD = 128
BLOCK = 128


MASKED = -1e30


def from_behind(value, axis, steps):
    count = lax.axis_size(axis)
    pairs = [(source, (source + steps) % count) for source in range(count)]
    return lax.ppermute(value, axis, pairs)


def block_rules(query_seq, key_seq, random_rows):
    nearby = key_seq[None, :] >= query_seq[:, None] - 2
    global_keys = key_seq[None, :] < 2
    drawn_keys = jnp.any(random_rows[:, :, None] == key_seq[None, None, :], axis=1)
    return nearby | global_keys | drawn_keys


def token_rules(block_ok, query_seq, key_seq, block_width):
    offsets = jnp.arange(block_width, dtype=jnp.int32)
    query_pos = (query_seq[:, None] * block_width + offsets[None, :]).reshape(-1)
    key_pos = (key_seq[:, None] * block_width + offsets[None, :]).reshape(-1)
    causal = key_pos[None, :] <= query_pos[:, None]
    spread = jnp.repeat(jnp.repeat(block_ok, block_width, axis=0), block_width, axis=1)
    return causal & spread


def local_rows(table, wanted, count):
    picks = (wanted[:, None] == jnp.arange(count, dtype=jnp.int32)[None, :]).astype(jnp.int32)
    return jnp.sum(picks[:, :, None] * table[None, :, :], axis=1)


def add_rows(first, second):
    return (first.astype(jnp.float32) + second.astype(jnp.float32)).astype(jnp.bfloat16)


def body(queries, keys, values, residual, rand_blocks, block_order):
    token_rows = queries.shape[1]
    local_blocks = token_rows // BLOCK
    order_here = block_order[0]
    total_blocks = order_here.shape[0]
    kv_heads = keys.shape[2] // HD
    groups = queries.shape[2] // keys.shape[2]
    factor = 1.0 / math.sqrt(HD)
    position = lax.axis_index("ctx")
    query_seq = lax.dynamic_slice_in_dim(order_here, position * local_blocks, local_blocks)
    random_here = local_rows(rand_blocks[0], query_seq, total_blocks)
    query_rows = queries[0].reshape(token_rows, kv_heads, groups, HD)
    start_state = (
        jnp.full((token_rows, kv_heads, groups), MASKED, jnp.float32),
        jnp.zeros((token_rows, kv_heads, groups), jnp.float32),
        jnp.zeros((token_rows, kv_heads, groups, HD), jnp.float32),
    )
    key_shard = lax.all_gather(keys, "ctx", axis=1, tiled=True)[0]
    value_shard = lax.all_gather(values, "ctx", axis=1, tiled=True)[0]
    shard_rows = key_shard.shape[0]
    tile_rows = math.gcd(shard_rows, 512)

    def one_tile(tile_step, state):
        row_max, row_total, weighted = state
        offset = tile_step * tile_rows
        key_tile = lax.dynamic_slice_in_dim(key_shard, offset, tile_rows, 0).reshape(
            tile_rows, kv_heads, HD
        )
        value_tile = lax.dynamic_slice_in_dim(value_shard, offset, tile_rows, 0).reshape(
            tile_rows, kv_heads, HD
        )
        key_seq = lax.dynamic_slice_in_dim(order_here, offset // BLOCK, tile_rows // BLOCK)
        block_ok = block_rules(query_seq, key_seq, random_here)
        allowed = token_rules(block_ok, query_seq, key_seq, BLOCK)[:, None, None, :]
        scores = (
            jnp.einsum("qkgd,rkd->qkgr", query_rows, key_tile, preferred_element_type=jnp.float32)
            * factor
        )
        scores = jnp.where(allowed, scores, MASKED)
        new_max = jnp.maximum(row_max, jnp.max(scores, axis=-1))
        weights = jnp.where(allowed, jnp.exp(scores - new_max[..., None]), 0.0)
        rescale = jnp.exp(row_max - new_max)
        row_total = row_total * rescale + jnp.sum(weights, axis=-1)
        update = jnp.einsum(
            "qkgr,rkd->qkgd",
            weights.astype(jnp.bfloat16),
            value_tile,
            preferred_element_type=jnp.float32,
        )
        weighted = weighted * rescale[..., None] + update
        return (new_max, row_total, weighted)

    final_max, final_total, final_weighted = lax.fori_loop(
        0, shard_rows // tile_rows, one_tile, start_state
    )
    mixed = final_weighted / final_total[..., None]
    attended = mixed.reshape(1, token_rows, queries.shape[2]).astype(jnp.bfloat16)
    received = from_behind(add_rows(attended, residual), "section", 1)
    return received


def solution(mesh):
    return jax.shard_map(
        body,
        mesh=mesh,
        in_specs=(
            P("section", "ctx", "tp"),
            P("section", "ctx", "tp"),
            P("section", "ctx", "tp"),
            P("section", "ctx", "tp"),
            P("section", None, None),
            P("section", None),
        ),
        out_specs=P("section", "ctx", "tp"),
        check_vma=False,
    )
```

profile of v0, /device:TPU:1, one launch (start us, length us, event | category | flops | bytes accessed | tf_op | source)
XLA Modules:
  0.0 184.0 jit_solution(14292785486286544493)
XLA Ops:
  6.5 1.7 copy.21
  8.3 1.7 copy.23
  10.0 0.7 copy.35
  10.7 0.7 dynamic-slice_bitcast_fusion
  11.4 0.1 compare_convert_fusion
  11.5 0.1 multiply_reduce_fusion
  11.6 0.1 copy.24
  11.7 1.5 copy.22
  13.2 0.7 copy.25
  13.9 30.2 %all-gather.3.cloned.1.call-done = bf16[1,2048,256]{1,2,0:T(8,128)(2,1)} async-done(((bf16[1,256,256]{1,2,0:T(8,128)(2,1)}), bf16[1,2048,256]{1,2,0:T(8,128)(2,1)}) %all-gather.3.cloned.1.call-update) | async-done | bytes 1048592 | tf_op jit(solution)/shard_map/all_gather | solution.py:63
  44.1 31.9 %all-gather.5.cloned.1.call-done = bf16[1,2048,256]{1,2,0:T(8,128)(2,1)} async-done(((bf16[1,256,256]{1,2,0:T(8,128)(2,1)}), bf16[1,2048,256]{1,2,0:T(8,128)(2,1)}) %all-gather.5.cloned.1.call-update) | async-done | bytes 1048592 | tf_op jit(solution)/shard_map/all_gather | solution.py:64
  75.9 39.6 %while.20 = (s32[]{:T(128)}, f32[256,2,8]{0,2,1:T(8,128)S(1)}, f32[256,2,8]{0,2,1:T(8,128)S(1)}, f32[256,2,8,128]{0,3,2,1:T(8,128)}, s32[16]{0:T(128)}, /*index=...) while((s32[]{:T(128)}, f32[256,2,8]{0,2,1:T(8,128)S(1)}, ...), condition=%wide.region_5.6_spmd.clone, body=%wide.region_1.5_spmd.clone.sunk | while | flops 1102861184 | bytes 49554092 | solution.py:98
  75.9 0.7 broadcast_compare_fusion.2
  76.7 0.1 compare_reduce_fusion.2
  76.8 0.1 or_or_fusion.2
  76.9 0.1 add_bitcast_fusion.4
  76.9 0.1 broadcast_bitcast_fusion.2
  77.0 0.1 add_bitcast_fusion.5
  77.1 0.2 bitcast_and_fusion.2
  77.2 1.1 constant_dynamic-slice_fusion.3
  78.3 1.5 fusion.26
  79.9 2.0 %fusion.27 = f32[256,2,8]{0,2,1:T(8,128)S(1)} fusion(f32[2,512,256,8]{2,1,3,0:T(8,128)S(1)} %get-tuple-element.412, f32[256,2,8]{0,2,1:T(8,128)S(1)} %select_maximum_fusion.2, pred[256,512]{0,1:T(8,128)(4,1)S(1)} %bitcast_and_fusion.2), kind=kLoop, calls=%fused_computation.4.clone.1 | loop fusion | flops 10481664 | bytes 8552448 | tf_op jit(solution)/shard_map/while/body/eval_jaxpr/reduce_sum | solution.py:88
  81.9 2.6 %bitcast_add_fusion.2 = f32[256,2,8,128]{0,3,2,1:T(8,128)S(1)} fusion(f32[256,2,8,128]{0,3,2,1:T(8,128)S(1)} %copy-done, bf16[512,2,128,1]{0,2,3,1:T(8,128)(2,1)S(1)} %bitcast.74, f32[2,512,256,8]{2,1,3,0:T(8,128)S(1)} %get-tuple-element.412, f32[256,2,8]{0,2,1:T(8,128)S(1)} %select_maximum_fusion.2, pred[256,512]{0,1:T(8,128)(4,1)S(1)} %bitcast_and_fusion.2, ...), kind=kOutput, calls=%fused_computation.7.clone.1 | convolution fusion | flops 548929536 | bytes 13008897 | tf_op jit(solution)/shard_map/while/body/eval_jaxpr/qkgr,rkd->qkgd/dot_general | solution.py:89
  84.5 1.3 copy-done.1
  85.8 0.7 broadcast_compare_fusion.2
  86.6 0.1 compare_reduce_fusion.2
  86.7 0.1 or_or_fusion.2
  86.8 0.1 add_bitcast_fusion.4
  86.8 0.1 broadcast_bitcast_fusion.2
  86.9 0.1 add_bitcast_fusion.5
  87.0 0.2 bitcast_and_fusion.2
  87.1 1.1 constant_dynamic-slice_fusion.3
  88.2 1.5 fusion.26
  89.8 2.0 %fusion.27 = f32[256,2,8]{0,2,1:T(8,128)S(1)} fusion(f32[2,512,256,8]{2,1,3,0:T(8,128)S(1)} %get-tuple-element.412, f32[256,2,8]{0,2,1:T(8,128)S(1)} %select_maximum_fusion.2, pred[256,512]{0,1:T(8,128)(4,1)S(1)} %bitcast_and_fusion.2), kind=kLoop, calls=%fused_computation.4.clone.1 | loop fusion | flops 10481664 | bytes 8552448 | tf_op jit(solution)/shard_map/while/body/eval_jaxpr/reduce_sum | solution.py:88
  91.8 2.6 %bitcast_add_fusion.2 = f32[256,2,8,128]{0,3,2,1:T(8,128)S(1)} fusion(f32[256,2,8,128]{0,3,2,1:T(8,128)S(1)} %copy-done, bf16[512,2,128,1]{0,2,3,1:T(8,128)(2,1)S(1)} %bitcast.74, f32[2,512,256,8]{2,1,3,0:T(8,128)S(1)} %get-tuple-element.412, f32[256,2,8]{0,2,1:T(8,128)S(1)} %select_maximum_fusion.2, pred[256,512]{0,1:T(8,128)(4,1)S(1)} %bitcast_and_fusion.2, ...), kind=kOutput, calls=%fused_computation.7.clone.1 | convolution fusion | flops 548929536 | bytes 13008897 | tf_op jit(solution)/shard_map/while/body/eval_jaxpr/qkgr,rkd->qkgd/dot_general | solution.py:89
  94.4 1.3 copy-done.1
  95.7 0.7 broadcast_compare_fusion.2
  96.5 0.1 compare_reduce_fusion.2
  96.6 0.1 or_or_fusion.2
  96.7 0.1 add_bitcast_fusion.4
  96.7 0.1 broadcast_bitcast_fusion.2
  96.9 0.2 bitcast_and_fusion.2
  97.0 1.1 constant_dynamic-slice_fusion.3
  98.1 1.5 fusion.26
  99.7 2.0 %fusion.27 = f32[256,2,8]{0,2,1:T(8,128)S(1)} fusion(f32[2,512,256,8]{2,1,3,0:T(8,128)S(1)} %get-tuple-element.412, f32[256,2,8]{0,2,1:T(8,128)S(1)} %select_maximum_fusion.2, pred[256,512]{0,1:T(8,128)(4,1)S(1)} %bitcast_and_fusion.2), kind=kLoop, calls=%fused_computation.4.clone.1 | loop fusion | flops 10481664 | bytes 8552448 | tf_op jit(solution)/shard_map/while/body/eval_jaxpr/reduce_sum | solution.py:88
  101.7 2.6 %bitcast_add_fusion.2 = f32[256,2,8,128]{0,3,2,1:T(8,128)S(1)} fusion(f32[256,2,8,128]{0,3,2,1:T(8,128)S(1)} %copy-done, bf16[512,2,128,1]{0,2,3,1:T(8,128)(2,1)S(1)} %bitcast.74, f32[2,512,256,8]{2,1,3,0:T(8,128)S(1)} %get-tuple-element.412, f32[256,2,8]{0,2,1:T(8,128)S(1)} %select_maximum_fusion.2, pred[256,512]{0,1:T(8,128)(4,1)S(1)} %bitcast_and_fusion.2, ...), kind=kOutput, calls=%fused_computation.7.clone.1 | convolution fusion | flops 548929536 | bytes 13008897 | tf_op jit(solution)/shard_map/while/body/eval_jaxpr/qkgr,rkd->qkgd/dot_general | solution.py:89
  104.3 1.3 copy-done.1
  105.7 0.7 broadcast_compare_fusion.2
  106.4 0.1 compare_reduce_fusion.2
  106.5 0.1 or_or_fusion.2
  106.6 0.1 add_bitcast_fusion.4
  106.6 0.1 broadcast_bitcast_fusion.2
  106.8 0.2 bitcast_and_fusion.2
  106.9 1.1 constant_dynamic-slice_fusion.3
  108.0 1.5 fusion.26
  109.6 2.0 %fusion.27 = f32[256,2,8]{0,2,1:T(8,128)S(1)} fusion(f32[2,512,256,8]{2,1,3,0:T(8,128)S(1)} %get-tuple-element.412, f32[256,2,8]{0,2,1:T(8,128)S(1)} %select_maximum_fusion.2, pred[256,512]{0,1:T(8,128)(4,1)S(1)} %bitcast_and_fusion.2), kind=kLoop, calls=%fused_computation.4.clone.1 | loop fusion | flops 10481664 | bytes 8552448 | tf_op jit(solution)/shard_map/while/body/eval_jaxpr/reduce_sum | solution.py:88
  111.6 2.6 %bitcast_add_fusion.2 = f32[256,2,8,128]{0,3,2,1:T(8,128)S(1)} fusion(f32[256,2,8,128]{0,3,2,1:T(8,128)S(1)} %copy-done, bf16[512,2,128,1]{0,2,3,1:T(8,128)(2,1)S(1)} %bitcast.74, f32[2,512,256,8]{2,1,3,0:T(8,128)S(1)} %get-tuple-element.412, f32[256,2,8]{0,2,1:T(8,128)S(1)} %select_maximum_fusion.2, pred[256,512]{0,1:T(8,128)(4,1)S(1)} %bitcast_and_fusion.2, ...), kind=kOutput, calls=%fused_computation.7.clone.1 | convolution fusion | flops 548929536 | bytes 13008897 | tf_op jit(solution)/shard_map/while/body/eval_jaxpr/qkgr,rkd->qkgd/dot_general | solution.py:89
  114.2 1.3 copy-done.1
  115.6 1.8 divide_convert_fusion
  117.4 0.6 copy.30
  118.0 1.5 add_convert_fusion
  119.5 3.3 %collective-permute-start = (bf16[1,256,2048]{2,1,0:T(8,128)(2,1)S(1)}, bf16[1,256,2048]{2,1,0:T(8,128)(2,1)S(1)}, u32[]{:S(2)}, u32[]{:S(2)}) collective-permute-start(bf16[1,256,2048]{2,1,0:T(8,128)(2,1)S(1)} %add_convert_fusion), channel_id=1, source_target_pairs={{0,32},{32,64},{64,96},{96,128},{128,160},{160,192},{192,224},{224... | collective-permute-start | bytes 3145736 | tf_op jit(solution)/shard_map/ppermute | solution.py:18
  122.8 53.4 %collective-permute-done = bf16[1,256,2048]{2,1,0:T(8,128)(2,1)S(1)} collective-permute-done((bf16[1,256,2048]{2,1,0:T(8,128)(2,1)S(1)}, bf16[1,256,2048]{2,1,0:T(8,128)(2,1)S(1)}, u32[]{:S(2)}, u32[]{:S(2)}) %collective-permute-start) | collective-permute-done | bytes 1048608 | tf_op jit(solution)/shard_map/ppermute | solution.py:18
  176.2 1.0 copy.49
  (41 shorter events, 0.4 us)
Async XLA Ops:
  6.5 37.5 %all-gather.3.cloned.1.call-start = ((), (), s32[]{:S(2)}) async-start(), calls=%async_computation | async-start | bytes 1179648 | tf_op jit(solution)/shard_map/all_gather | solution.py:63
  8.2 67.7 %all-gather.5.cloned.1.call-start = ((), (), s32[]{:S(2)}) async-start(), calls=%async_computation.1 | async-start | bytes 1179648 | tf_op jit(solution)/shard_map/all_gather | solution.py:64
  78.3 3.6 %copy-start = (f32[256,2,8,128]{0,3,2,1:T(8,128)S(1)}, f32[256,2,8,128]{0,3,2,1:T(8,128)}, u32[]{:S(2)}) copy-start(f32[256,2,8,128]{0,3,2,1:T(8,128)} %get-tuple-element.437) | copy-start | bytes 6291460 | tf_op jit(solution)/shard_map/while
  84.5 1.3 copy-start.1
  88.2 3.6 %copy-start = (f32[256,2,8,128]{0,3,2,1:T(8,128)S(1)}, f32[256,2,8,128]{0,3,2,1:T(8,128)}, u32[]{:S(2)}) copy-start(f32[256,2,8,128]{0,3,2,1:T(8,128)} %get-tuple-element.437) | copy-start | bytes 6291460 | tf_op jit(solution)/shard_map/while
  94.4 1.3 copy-start.1
  98.1 3.6 %copy-start = (f32[256,2,8,128]{0,3,2,1:T(8,128)S(1)}, f32[256,2,8,128]{0,3,2,1:T(8,128)}, u32[]{:S(2)}) copy-start(f32[256,2,8,128]{0,3,2,1:T(8,128)} %get-tuple-element.437) | copy-start | bytes 6291460 | tf_op jit(solution)/shard_map/while
  104.3 1.3 copy-start.1
  108.0 3.6 %copy-start = (f32[256,2,8,128]{0,3,2,1:T(8,128)S(1)}, f32[256,2,8,128]{0,3,2,1:T(8,128)}, u32[]{:S(2)}) copy-start(f32[256,2,8,128]{0,3,2,1:T(8,128)} %get-tuple-element.437) | copy-start | bytes 6291460 | tf_op jit(solution)/shard_map/while
  114.2 1.3 copy-start.1
  119.5 56.6 %collective-permute-start = (bf16[1,256,2048]{2,1,0:T(8,128)(2,1)S(1)}, bf16[1,256,2048]{2,1,0:T(8,128)(2,1)S(1)}, u32[]{:S(2)}, u32[]{:S(2)}) collective-permute-start(bf16[1,256,2048]{2,1,0:T(8,128)(2,1)S(1)} %add_convert_fusion), channel_id=1, source_target_pairs={{0,32},{32,64},{64,96},{96,128},{128,160},{160,192},{192,224},{224... | collective-permute-start | bytes 3145736 | tf_op jit(solution)/shard_map/ppermute | solution.py:18
Sparse Core Ops, SparseCore 0:
  9.5 34.5 all-gather.2
  46.2 29.7 all-gather.4
where the time goes:
time: 184 us
  waiting for transfers between devices  115 us (62%)
  local copies, waits for them, and re-layouts  18.5 us (10%)
  matrix products  16.5 us (9%)
  other arithmetic  16.4 us (9%)
  between operations  13.5 us (7%)
  starting transfers between devices  3.32 us (2%)
    ppermute x1, waiting for transfers between devices, from_behind(): return lax.ppermute(value, axis, pairs)  53.4 us
    all_gather x1, waiting for transfers between devices, body(): value_shard = lax.all_gather(values, 'ctx', axis=1, tiled=True)[0]  31.9 us
    all_gather x1, waiting for transfers between devices, body(): key_shard = lax.all_gather(keys, 'ctx', axis=1, tiled=True)[0]  30.2 us
    dot_general x4, matrix products, one_tile(): jnp.einsum('qkgr,rkd->qkgd', weights.astype(jnp.bfloat16), value_tile, pr...  10.4 us
    reduce_sum x4, other arithmetic, one_tile(): row_total = row_total * rescale + jnp.sum(weights, axis=-1)  8.02 us
    unnamed x7, local copies, waits for them, and re-layouts  7.22 us
    dot_general x4, matrix products, one_tile(): jnp.einsum('qkgd,rkd->qkgr', query_rows, key_tile, preferred_element_type...  6.08 us
    while x20, local copies, waits for them, and re-layouts  5.28 us
  transfers between devices with their start and end apart: 3, of which 3 were waited for; matrix products, arithmetic and copies ran while one was open for 3% of the time, Pallas kernels for 0%

commit v1 on v0

v1 whole, which is shorter than its diff:
```python
import functools
import math

import jax
import jax.numpy as jnp
from jax import lax
from jax.experimental import pallas as pl
from jax.experimental.pallas import tpu as pltpu
from jax.sharding import PartitionSpec as P

MESH = pl.DeviceIdType.MESH
HD = 128
BLOCK = 128
SLOTS = 8
MASKED = -1e30
CHUNKS = 8
HEADS = 4
SIDES = 2
LEFT0, LEFT1, RIGHT1, RIGHT0, SIB, OPP0, OPP1, SIB_LEFT, SIB_RIGHT, SIB_OPP0, SIB_OPP1 = range(11)
PIECES = 11
MID_LAST = False


def kernel(
    zs, ys, q_hbm, k_hbm, v_hbm, r_hbm, rand_ref, order_ref, out_ref,
    kv0, kv1, q_v, r_v, o_v, ksel, vsel, relay, slot_at, slot_ok,
    load_sem, piece_send, piece_recv, out_send, out_recv, mid_recv, mid_send,
):
    kv = (kv0, kv1)
    section, ctx, tp = lax.axis_index("section"), lax.axis_index("ctx"), lax.axis_index("tp")
    tps = ys // 2
    chips = lax.axis_size("ctx") // 2
    z, y = section % zs, (section // zs) * tps + tp
    x, core = ctx // 2, ctx % 2
    left, right = (x + chips - 1) % chips, (x + 1) % chips
    opp = (x + 2) % chips

    def at(chip, c):
        return chip * 2 + c

    def dev_ctx(chip, c):
        return (section, at(chip, c), tp)

    def dev_yz(y2, z2):
        y2 = (y2 + ys) % ys
        return ((y2 // tps) * zs + z2, ctx, y2 % tps)

    sib_dev, left_dev, right_dev = dev_ctx(x, 1 - core), dev_ctx(left, core), dev_ctx(right, core)
    first, last = z == 0, z == zs - 1
    mid = last if MID_LAST else first
    mid_z = zs - 1 if MID_LAST else 0

    own = pl.ds(2 * ctx, 2)
    kv_loads = []
    for h in range(2):
        cols = pl.ds(h * HD, HD)
        for which, src in enumerate((k_hbm, v_hbm)):
            kv_loads.append(
                pltpu.make_async_copy(src.at[:, :, cols], kv[h].at[own, which], load_sem.at[2 * h + which])
            )
    q_load = pltpu.make_async_copy(q_hbm, q_v, load_sem.at[4])
    r_load = pltpu.make_async_copy(r_hbm, r_v, load_sem.at[5])
    for copy in (*kv_loads, q_load, r_load):
        copy.start()

    barrier = pltpu.get_barrier_semaphore()

    def greet(dev):
        pl.semaphore_signal(barrier, inc=1, device_id=dev, device_id_type=MESH)

    greet(sib_dev)
    greet(left_dev)
    greet(right_dev)

    @pl.when(z > 0)
    def _():
        greet((section - 1, ctx, tp))

    if MID_LAST:
        @pl.when(first)
        def _():
            greet(dev_yz(y + 2, zs - 1))
            greet(dev_yz(y - 2, zs - 1))

        @pl.when(last)
        def _():
            greet(dev_yz(y + 2, zs - 1))
            greet(dev_yz(y - 2, zs - 1))
    else:
        @pl.when(first)
        def _():
            greet(dev_yz(y + 2, zs - 1))
            greet(dev_yz(y - 2, zs - 1))
            greet(dev_yz(y + 2, 0))
            greet(dev_yz(y - 2, 0))

    for here, count in ((first, 4 if MID_LAST else 6), (last, 7 if MID_LAST else 5), (~first & ~last, 4)):
        @pl.when(here)
        def _(count=count):
            pl.semaphore_wait(barrier, count)

    def piece(h, tag, blocks, dev):
        part = kv[h].at[blocks]
        return pltpu.make_async_remote_copy(
            src_ref=part, dst_ref=part, send_sem=piece_send.at[h, tag], recv_sem=piece_recv.at[h, tag],
            device_id=dev, device_id_type=MESH,
        )

    def one(chip, c, b):
        return pl.ds(2 * at(chip, c) + b, 1)

    def two(chip, c):
        return pl.ds(2 * at(chip, c), 2)

    sent = {
        LEFT0: (one(x, core, 0), right_dev),
        LEFT1: (one(x, core, 1), right_dev),
        RIGHT1: (one(x, core, 1), left_dev),
        RIGHT0: (one(x, core, 0), left_dev),
        SIB: (two(x, core), sib_dev),
        OPP0: (one(left, core, 0), right_dev),
        OPP1: (one(right, core, 1), left_dev),
        SIB_LEFT: (two(left, core), sib_dev),
        SIB_RIGHT: (two(right, core), sib_dev),
        SIB_OPP0: (one(opp, core, 0), sib_dev),
        SIB_OPP1: (one(opp, core, 1), sib_dev),
    }
    received = {
        LEFT0: (one(left, core, 0), right_dev),
        LEFT1: (one(left, core, 1), right_dev),
        RIGHT1: (one(right, core, 1), left_dev),
        RIGHT0: (one(right, core, 0), left_dev),
        SIB: (two(x, 1 - core), sib_dev),
        OPP0: (one(opp, core, 0), right_dev),
        OPP1: (one(opp, core, 1), left_dev),
        SIB_LEFT: (two(left, 1 - core), sib_dev),
        SIB_RIGHT: (two(right, 1 - core), sib_dev),
        SIB_OPP0: (one(opp, 1 - core, 0), sib_dev),
        SIB_OPP1: (one(opp, 1 - core, 1), sib_dev),
    }

    def send(h, tag):
        return piece(h, tag, *sent[tag])

    def await_piece(h, tag):
        piece(h, tag, *received[tag]).wait_recv()

    def send_own(h):
        for tag in (LEFT0, RIGHT1, LEFT1, RIGHT0, SIB):
            send(h, tag).start()

    def send_far(h):
        await_piece(h, LEFT0)
        send(h, OPP0).start()
        await_piece(h, RIGHT1)
        send(h, OPP1).start()

    def send_sib(h):
        await_piece(h, LEFT1)
        send(h, SIB_LEFT).start()
        await_piece(h, RIGHT0)
        send(h, SIB_RIGHT).start()
        await_piece(h, OPP0)
        send(h, SIB_OPP0).start()
        await_piece(h, OPP1)
        send(h, SIB_OPP1).start()

    def arrive(h):
        for tag in (SIB, SIB_LEFT, SIB_RIGHT, SIB_OPP0, SIB_OPP1):
            await_piece(h, tag)

    kv_loads[0].wait()
    kv_loads[1].wait()
    send_own(0)
    kv_loads[2].wait()
    kv_loads[3].wait()

    for b in range(2):
        i = order_ref[0, 2 * ctx + b]
        rand = [rand_ref[r, 0, i] for r in range(3)]
        wanted = [i, i - 1, i - 2, 0, 1, *rand]
        far = [(rand[r] < i - 2) & (rand[r] >= 2) for r in range(3)]
        valid = [
            i >= 0, i >= 1, i >= 2, i >= 3, i >= 4,
            far[0], far[1] & (rand[1] != rand[0]), far[2] & (rand[2] != rand[0]) & (rand[2] != rand[1]),
        ]
        places = [jnp.int32(0)] * SLOTS
        for p in range(16):
            held = order_ref[0, p]
            places = [jnp.where(held == j, p, place) for j, place in zip(wanted, places)]
        for s in range(SLOTS):
            slot_at[b, s] = places[s]
            slot_ok[b, s] = jnp.where(valid[s], 1, 0)

    send_far(0)
    send_own(1)
    send_sib(0)
    q_load.wait()
    arrive(0)
    r_load.wait()

    def pick(h):
        for b in range(2):
            for s in range(SLOTS):
                place = slot_at[b, s]
                ksel[b, pl.ds(s * BLOCK, BLOCK), :] = kv[h][place, 0]
                vsel[b, pl.ds(s * BLOCK, BLOCK), :] = kv[h][place, 1]

    scale = math.log2(math.e) / math.sqrt(HD)

    def where_out(c, d):
        h, b, half = c // 4, (c // 2) % 2, c % 2
        cols = (h * 2 + half) * (HEADS * HD) + d * (HEADS * HD // 2)
        return pl.ds(pl.multiple_of(b * BLOCK, BLOCK), BLOCK), pl.ds(pl.multiple_of(cols, 2 * HD), 2 * HD)

    def to_next(c, d):
        rows, cols = where_out(c, d)
        return pltpu.make_async_remote_copy(
            src_ref=o_v.at[rows, cols], dst_ref=out_ref.at[rows, cols],
            send_sem=out_send.at[c, d], recv_sem=out_recv.at[c, d],
            device_id=(section + 1, ctx, tp), device_id_type=MESH,
        )

    def to_mid(c, d):
        rows, cols = where_out(c, d)
        return pltpu.make_async_remote_copy(
            src_ref=o_v.at[rows, cols], dst_ref=relay.at[d, c],
            send_sem=out_send.at[c, d], recv_sem=mid_recv.at[c, d],
            device_id=dev_yz(y + 2 - 4 * d, mid_z), device_id_type=MESH,
        )

    def from_mid(c, d):
        rows, cols = where_out(c, d)
        return pltpu.make_async_remote_copy(
            src_ref=relay.at[d, c], dst_ref=out_ref.at[rows, cols],
            send_sem=mid_send.at[c, d], recv_sem=out_recv.at[c, d],
            device_id=dev_yz(y + 2 - 4 * d, 0), device_id_type=MESH,
        )

    def pass_on(c):
        for d in range(SIDES):
            to_mid(c, d).wait_recv()
            from_mid(c, d).start()

    def chunk(c, carry):
        h, b, half = c // 4, (c // 2) % 2, c % 2

        @pl.when(c == 0)
        def _():
            pick(0)

        @pl.when(c == 1)
        def _():
            send_far(1)

        @pl.when(c == 2)
        def _():
            send_sib(1)

        @pl.when(c == 4)
        def _():
            arrive(1)
            pick(1)

        rows = pl.ds(pl.multiple_of(b * BLOCK, BLOCK), BLOCK)
        start = (h * 2 + half) * (HEADS * HD)
        cols = [pl.ds(pl.multiple_of(start + g * HD, HD), HD) for g in range(HEADS)]
        keys, vals = ksel[b], vsel[b]
        bias = [jnp.where(slot_ok[b, s] > 0, 0.0, MASKED) for s in range(SLOTS)]
        row_at = lax.broadcasted_iota(jnp.int32, (BLOCK, BLOCK), 0)
        key_at = lax.broadcasted_iota(jnp.int32, (BLOCK, BLOCK), 1)
        causal = key_at <= row_at
        for g in range(HEADS):
            scores = lax.dot_general(
                q_v[rows, cols[g]], keys, (((1,), (1,)), ((), ())), preferred_element_type=jnp.float32
            )
            parts = [scores[:, s * BLOCK : (s + 1) * BLOCK] for s in range(SLOTS)]
            parts = [jnp.where(causal, parts[0], MASKED)] + [parts[s] + bias[s] for s in range(1, SLOTS)]
            top = functools.reduce(jnp.maximum, parts)
            top = jnp.max(top, axis=1, keepdims=True)
            weights = [jnp.exp2((part - top) * scale) for part in parts]
            total = jnp.sum(functools.reduce(jnp.add, weights), axis=1, keepdims=True)
            packed = jnp.concatenate([w.astype(jnp.bfloat16) for w in weights], axis=1)
            mixed = jnp.dot(packed, vals, preferred_element_type=jnp.float32) / total
            attended = mixed.astype(jnp.bfloat16).astype(jnp.float32)
            o_v[rows, cols[g]] = (attended + r_v[rows, cols[g]].astype(jnp.float32)).astype(jnp.bfloat16)

        @pl.when(z < zs - 1)
        def _():
            for d in range(SIDES):
                to_next(c, d).start()

        @pl.when(last)
        def _():
            for d in range(SIDES):
                to_mid(c, d).start()

        @pl.when(mid & (c >= 6))
        def _():
            pass_on(c - 6)

        return carry

    lax.fori_loop(0, CHUNKS, chunk, 0)

    @pl.when(mid)
    def _():
        def later(c, carry):
            pass_on(c)
            return carry

        lax.fori_loop(2, CHUNKS, later, 0)

    def finish(c, carry):
        for d in range(SIDES):
            to_next(c, d).wait_recv()
            to_next(c, d).wait_send()
        return carry

    lax.fori_loop(0, CHUNKS, finish, 0)

    @pl.when(mid)
    def _():
        def passed(c, carry):
            for d in range(SIDES):
                from_mid(c, d).wait_send()
            return carry

        lax.fori_loop(0, CHUNKS, passed, 0)

    for h in range(2):
        for tag in range(PIECES):
            send(h, tag).wait_send()


def solution(mesh):
    zs = mesh.shape["section"] // 2
    ys = mesh.shape["tp"] * 2

    def body(queries, keys, values, residual, rand_blocks, block_order):
        _, rows, width = queries.shape
        kv_width = keys.shape[2]
        hbm, smem = pl.BlockSpec(memory_space=pl.ANY), pl.BlockSpec(memory_space=pltpu.SMEM)
        blocks = 2 * mesh.shape["ctx"]
        dma = pltpu.SemaphoreType.DMA
        out = pl.pallas_call(
            functools.partial(kernel, zs, ys),
            out_shape=jax.ShapeDtypeStruct((rows, width), jnp.bfloat16),
            in_specs=[hbm, hbm, hbm, hbm, smem, smem],
            out_specs=hbm,
            scratch_shapes=[
                pltpu.VMEM((blocks, 2, BLOCK, HD), jnp.bfloat16),
                pltpu.VMEM((blocks, 2, BLOCK, HD), jnp.bfloat16),
                pltpu.VMEM((rows, width), jnp.bfloat16),
                pltpu.VMEM((rows, width), jnp.bfloat16),
                pltpu.VMEM((rows, width), jnp.bfloat16),
                pltpu.VMEM((2, SLOTS * BLOCK, HD), jnp.bfloat16),
                pltpu.VMEM((2, SLOTS * BLOCK, HD), jnp.bfloat16),
                pltpu.VMEM((SIDES, CHUNKS, BLOCK, 2 * HD), jnp.bfloat16),
                pltpu.SMEM((2, SLOTS), jnp.int32),
                pltpu.SMEM((2, SLOTS), jnp.int32),
                dma((6,)),
                dma((2, PIECES)),
                dma((2, PIECES)),
                dma((CHUNKS, SIDES)),
                dma((CHUNKS, SIDES)),
                dma((CHUNKS, SIDES)),
                dma((CHUNKS, SIDES)),
            ],
            compiler_params=pltpu.CompilerParams(
                collective_id=0, has_side_effects=True, vmem_limit_bytes=56 * 1024 * 1024
            ),
        )(
            queries.reshape(rows, width),
            keys.reshape(rows // BLOCK, BLOCK, kv_width),
            values.reshape(rows // BLOCK, BLOCK, kv_width),
            residual.reshape(rows, width),
            rand_blocks.transpose(2, 0, 1),
            block_order,
        )
        return out.reshape(1, rows, width)

    spec = P("section", "ctx", "tp")
    return jax.shard_map(
        body,
        mesh=mesh,
        in_specs=(spec, spec, spec, spec, P("section", None, None), P("section", None)),
        out_specs=spec,
        check_vma=False,
    )
```

time: 184 us -> 62.6 us (0.34)
  waiting for transfers between devices: 115 us -> 0 us
  Pallas kernels: 0 us -> 60.1 us
  matrix products: 16.5 us -> 0 us
  other arithmetic: 16.4 us -> 0 us
  local copies, waits for them, and re-layouts: 18.5 us -> 2.3 us
  between operations: 13.5 us -> 0.01 us
  starting transfers between devices: 3.32 us -> 0 us
    all_gather x2 -> x0, waiting for transfers between devices: 62.1 us -> none  [the longest x1 31.9 us: body(): value_shard = lax.all_gather(values, 'ctx', axis=1, tiled=True)[0]]
    pallas_call x0 -> x1, Pallas kernels: none -> 60.1 us  [body(): pl.pallas_call(functools.partial(kernel, zs, ys), out_shape=jax.ShapeDtyp...]
    ppermute x1 -> x0, waiting for transfers between devices: 53.4 us -> none  [from_behind(): return lax.ppermute(value, axis, pairs)]
    dot_general x8 -> x0, matrix products: 16.5 us -> none  [the longest x4 10.4 us: one_tile(): jnp.einsum('qkgr,rkd->qkgd', weights.astype(jnp.bfloat16), value_tile, pr...]
    reduce_sum x5 -> x0, other arithmetic: 8.16 us -> none  [the longest x4 8.02 us: one_tile(): row_total = row_total * rescale + jnp.sum(weights, axis=-1)]
    while x20 -> x0, local copies, waits for them, and re-layouts: 5.28 us -> none
    dynamic_slice x5 -> x0, local copies, waits for them, and re-layouts: 5.02 us -> none  [the longest x4 4.29 us: one_tile(): lax.dynamic_slice_in_dim(value_shard, offset, tile_rows, 0)]
    unnamed x7 -> x1, local copies, waits for them, and re-layouts: 7.22 us -> 2.3 us
  transfers between devices with their start and end apart: 3 -> 0, of which waited for: 3 -> 0; matrix products, arithmetic and copies ran while one was open for 3% -> 0% of each run, Pallas kernels for 0% -> 0%
where the time goes in v1:
time: 62.6 us; the launch traced here: 62.4 us
  Pallas kernels  60.1 us (96%)
  local copies, waits for them, and re-layouts  2.3 us (4%)
    pallas_call x1, Pallas kernels, body(): pl.pallas_call(functools.partial(kernel, zs, ys), out_shape=jax.ShapeDtyp...  60.1 us
    unnamed x1, local copies, waits for them, and re-layouts  2.3 us

profile of v1, /device:TPU:1, one launch (start us, length us, event | category | flops | bytes accessed | tf_op | source)
XLA Modules:
  0.0 62.4 jit_solution(9916359268552178774)
XLA Ops:
  0.0 60.1 %shard_map.64 = bf16[256,2048]{1,0:T(8,128)(2,1)} custom-call(bf16[256,2048]{1,0:T(8,128)(2,1)} %bitcast.7, bf16[2,128,256]{2,1,0:T(8,128)(2,1)} %bitcast.9, bf16[2,128,256]{2,1,0:T(8,128)(2,1)} %bitcast.10, bf16[256,2048]{1,0:T(8,128)(2,1)} %bitcast.8, s32[3,1,16]{2,1,0:T(1,128)} %bitcast.11, s32[1,16]{1,0:T(1,128)} %order_ref.1), custom_call_target="tpu_custom_call" | custom-call | tf_op jit(solution)/shard_map/pallas_call | solution.py:346
  60.1 2.3 %copy.8 = bf16[1,256,2048]{2,1,0:T(8,128)(2,1)} copy(bf16[1,256,2048]{2,1,0:T(8,128)(2,1)} %bitcast.6) | data formatting | bytes 2097152

commit v2 on v1

--- a/solution.py
+++ b/solution.py
@@ -18,8 +18,44 @@
 SIDES = 2
 LEFT0, LEFT1, RIGHT1, RIGHT0, SIB, OPP0, OPP1, SIB_LEFT, SIB_RIGHT, SIB_OPP0, SIB_OPP1 = range(11)
 PIECES = 11
-MID_LAST = False
-
+HIGH, LOW = 5, 2
+
+
+def back(way):
+    return ((0, HIGH), (2 * way, LOW), (4 * way, 0))
+
+
+def turn(way):
+    return ((2 * way, 0), (4 * way, 0))
+
+
+def paths_of_units():
+    down, up = turn(1), turn(-1)
+    pairs = [
+        (back(1), down), (back(-1), up), (back(1), down), (back(-1), up),
+        (back(1), down), (back(-1), up), (down, up), (down, up),
+    ]
+    return {(c, d): pairs[c][d] for c in range(CHUNKS) for d in range(SIDES)}
+
+
+PATHS = paths_of_units()
+EARLY = {HIGH: 4}
+
+
+def hands_on(plane):
+    return [
+        (c, d, path[i], path[i + 1], i + 2 == len(path))
+        for (c, d), path in PATHS.items()
+        for i in range(len(path) - 1)
+        if path[i][1] == plane
+    ]
+
+
+def legs(plane, last):
+    out = [(there[0] - here[0], there[1]) for _, _, here, there, _ in hands_on(plane)]
+    if plane == last:
+        out += [path[0] for path in PATHS.values()]
+    return sorted(set(out))
 
 def kernel(
     zs, ys, q_hbm, k_hbm, v_hbm, r_hbm, rand_ref, order_ref, out_ref,
@@ -47,9 +83,6 @@
 
     sib_dev, left_dev, right_dev = dev_ctx(x, 1 - core), dev_ctx(left, core), dev_ctx(right, core)
     first, last = z == 0, z == zs - 1
-    mid = last if MID_LAST else first
-    mid_z = zs - 1 if MID_LAST else 0
-
     own = pl.ds(2 * ctx, 2)
     kv_loads = []
     for h in range(2):
@@ -76,27 +109,14 @@
     def _():
         greet((section - 1, ctx, tp))
 
-    if MID_LAST:
-        @pl.when(first)
-        def _():
-            greet(dev_yz(y + 2, zs - 1))
-            greet(dev_yz(y - 2, zs - 1))
-
-        @pl.when(last)
-        def _():
-            greet(dev_yz(y + 2, zs - 1))
-            greet(dev_yz(y - 2, zs - 1))
-    else:
-        @pl.when(first)
-        def _():
-            greet(dev_yz(y + 2, zs - 1))
-            greet(dev_yz(y - 2, zs - 1))
-            greet(dev_yz(y + 2, 0))
-            greet(dev_yz(y - 2, 0))
-
-    for here, count in ((first, 4 if MID_LAST else 6), (last, 7 if MID_LAST else 5), (~first & ~last, 4)):
-        @pl.when(here)
-        def _(count=count):
+    for plane in range(zs):
+        sources = [(step, source) for source in range(zs) for step, target in legs(source, zs - 1) if target == plane]
+        count = 3 + (plane < zs - 1) + len(legs(plane, zs - 1))
+
+        @pl.when(z == plane)
+        def _(sources=sources, count=count):
+            for step, source in sources:
+                greet(dev_yz(y - step, source))
             pl.semaphore_wait(barrier, count)
 
     def piece(h, tag, blocks, dev):
@@ -199,12 +219,16 @@
     arrive(0)
     r_load.wait()
 
-    def pick(h):
-        for b in range(2):
-            for s in range(SLOTS):
-                place = slot_at[b, s]
-                ksel[b, pl.ds(s * BLOCK, BLOCK), :] = kv[h][place, 0]
-                vsel[b, pl.ds(s * BLOCK, BLOCK), :] = kv[h][place, 1]
+    def pick(h, b):
+        token0 = kv[h][slot_at[b, 3], 0, pl.ds(0, 16), :].astype(jnp.float32)[:1]
+        spare = jnp.broadcast_to(token0, (BLOCK, HD)).astype(jnp.bfloat16)
+        ones, zeros = jnp.ones((BLOCK, HD), jnp.bfloat16), jnp.zeros((BLOCK, HD), jnp.bfloat16)
+        for s in range(SLOTS):
+            place, rows = slot_at[b, s], pl.ds(s * BLOCK, BLOCK)
+            ok = slot_ok[b, s] > 0
+            ksel[rows, :] = jnp.where(ok, kv[h][place, 0], spare)
+            vsel[rows, pl.ds(0, HD)] = jnp.where(ok, kv[h][place, 1], zeros)
+            vsel[rows, pl.ds(HD, HD)] = jnp.where(ok, ones, zeros)
 
     scale = math.log2(math.e) / math.sqrt(HD)
 
@@ -221,33 +245,30 @@
             device_id=(section + 1, ctx, tp), device_id_type=MESH,
         )
 
-    def to_mid(c, d):
-        rows, cols = where_out(c, d)
+    def unit(c, d, src, dst, send_sem, recv_sem, step, plane):
         return pltpu.make_async_remote_copy(
-            src_ref=o_v.at[rows, cols], dst_ref=relay.at[d, c],
-            send_sem=out_send.at[c, d], recv_sem=mid_recv.at[c, d],
-            device_id=dev_yz(y + 2 - 4 * d, mid_z), device_id_type=MESH,
+            src_ref=src, dst_ref=dst, send_sem=send_sem.at[c, d], recv_sem=recv_sem.at[c, d],
+            device_id=dev_yz(y + step, plane), device_id_type=MESH,
         )
 
-    def from_mid(c, d):
-        rows, cols = where_out(c, d)
-        return pltpu.make_async_remote_copy(
-            src_ref=relay.at[d, c], dst_ref=out_ref.at[rows, cols],
-            send_sem=mid_send.at[c, d], recv_sem=out_recv.at[c, d],
-            device_id=dev_yz(y + 2 - 4 * d, 0), device_id_type=MESH,
-        )
-
-    def pass_on(c):
-        for d in range(SIDES):
-            to_mid(c, d).wait_recv()
-            from_mid(c, d).start()
+    def first_leg(c, d):
+        path, (rows, cols) = PATHS[c, d], where_out(c, d)
+        if len(path) == 1:
+            return unit(c, d, o_v.at[rows, cols], out_ref.at[rows, cols], out_send, out_recv, *path[0])
+        return unit(c, d, o_v.at[rows, cols], relay.at[c, d], out_send, mid_recv, *path[0])
+
+    def next_leg(c, d, here, there, ends):
+        step, plane, (rows, cols) = there[0] - here[0], there[1], where_out(c, d)
+        if ends:
+            return unit(c, d, relay.at[c, d], out_ref.at[rows, cols], mid_send, out_recv, step, plane)
+        return unit(c, d, relay.at[c, d], relay.at[c, d], mid_send, mid_recv, step, plane)
+
+    def hand_on(c, d, here, there, ends):
+        unit(c, d, relay.at[c, d], relay.at[c, d], mid_send, mid_recv, 0, 0).wait_recv()
+        next_leg(c, d, here, there, ends).start()
 
     def chunk(c, carry):
         h, b, half = c // 4, (c // 2) % 2, c % 2
-
-        @pl.when(c == 0)
-        def _():
-            pick(0)
 
         @pl.when(c == 1)
         def _():
@@ -260,29 +281,36 @@
         @pl.when(c == 4)
         def _():
             arrive(1)
-            pick(1)
+
+        for key_head in range(2):
+            @pl.when((h == key_head) & (half == 0))
+            def _(key_head=key_head):
+                pick(key_head, b)
 
         rows = pl.ds(pl.multiple_of(b * BLOCK, BLOCK), BLOCK)
         start = (h * 2 + half) * (HEADS * HD)
         cols = [pl.ds(pl.multiple_of(start + g * HD, HD), HD) for g in range(HEADS)]
-        keys, vals = ksel[b], vsel[b]
-        bias = [jnp.where(slot_ok[b, s] > 0, 0.0, MASKED) for s in range(SLOTS)]
         row_at = lax.broadcasted_iota(jnp.int32, (BLOCK, BLOCK), 0)
         key_at = lax.broadcasted_iota(jnp.int32, (BLOCK, BLOCK), 1)
         causal = key_at <= row_at
-        for g in range(HEADS):
-            scores = lax.dot_general(
+        keys, vals = ksel[...], vsel[...]
+        scores = [
+            lax.dot_general(
                 q_v[rows, cols[g]], keys, (((1,), (1,)), ((), ())), preferred_element_type=jnp.float32
             )
-            parts = [scores[:, s * BLOCK : (s + 1) * BLOCK] for s in range(SLOTS)]
-            parts = [jnp.where(causal, parts[0], MASKED)] + [parts[s] + bias[s] for s in range(1, SLOTS)]
-            top = functools.reduce(jnp.maximum, parts)
-            top = jnp.max(top, axis=1, keepdims=True)
-            weights = [jnp.exp2((part - top) * scale) for part in parts]
-            total = jnp.sum(functools.reduce(jnp.add, weights), axis=1, keepdims=True)
-            packed = jnp.concatenate([w.astype(jnp.bfloat16) for w in weights], axis=1)
-            mixed = jnp.dot(packed, vals, preferred_element_type=jnp.float32) / total
-            attended = mixed.astype(jnp.bfloat16).astype(jnp.float32)
+            for g in range(HEADS)
+        ]
+        weights = []
+        for score in scores:
+            parts = [score[:, s * BLOCK : (s + 1) * BLOCK] for s in range(SLOTS)]
+            parts[0] = jnp.where(causal, parts[0], MASKED)
+            top = jnp.max(functools.reduce(jnp.maximum, parts), axis=1, keepdims=True)
+            weights.append(
+                jnp.concatenate([jnp.exp2((part - top) * scale).astype(jnp.bfloat16) for part in parts], axis=1)
+            )
+        for g in range(HEADS):
+            mixed = jnp.dot(weights[g], vals, preferred_element_type=jnp.float32)
+            attended = (mixed[:, :HD] / mixed[:, HD:]).astype(jnp.bfloat16).astype(jnp.float32)
             o_v[rows, cols[g]] = (attended + r_v[rows, cols[g]].astype(jnp.float32)).astype(jnp.bfloat16)
 
         @pl.when(z < zs - 1)
@@ -290,26 +318,30 @@
             for d in range(SIDES):
                 to_next(c, d).start()
 
-        @pl.when(last)
-        def _():
-            for d in range(SIDES):
-                to_mid(c, d).start()
-
-        @pl.when(mid & (c >= 6))
-        def _():
-            pass_on(c - 6)
+        for k in range(CHUNKS):
+            @pl.when(last & (c == k))
+            def _(k=k):
+                for d in range(SIDES):
+                    first_leg(k, d).start()
+
+        for plane, lag in EARLY.items():
+            for move in hands_on(plane):
+                if move[0] + lag < CHUNKS:
+                    @pl.when((z == plane) & (c == move[0] + lag))
+                    def _(move=move):
+                        hand_on(*move)
 
         return carry
 
     lax.fori_loop(0, CHUNKS, chunk, 0)
 
-    @pl.when(mid)
-    def _():
-        def later(c, carry):
-            pass_on(c)
-            return carry
-
-        lax.fori_loop(2, CHUNKS, later, 0)
+    for plane in range(zs):
+        moves = [m for m in hands_on(plane) if plane not in EARLY or m[0] + EARLY[plane] >= CHUNKS]
+        if moves:
+            @pl.when(z == plane)
+            def _(moves=moves):
+                for move in moves:
+                    hand_on(*move)
 
     def finish(c, carry):
         for d in range(SIDES):
@@ -319,14 +351,12 @@
 
     lax.fori_loop(0, CHUNKS, finish, 0)
 
-    @pl.when(mid)
-    def _():
-        def passed(c, carry):
-            for d in range(SIDES):
-                from_mid(c, d).wait_send()
-            return carry
-
-        lax.fori_loop(0, CHUNKS, passed, 0)
+    for plane in range(zs):
+        if hands_on(plane):
+            @pl.when(z == plane)
+            def _(plane=plane):
+                for move in hands_on(plane):
+                    next_leg(*move).wait_send()
 
     for h in range(2):
         for tag in range(PIECES):
@@ -345,18 +375,18 @@
         dma = pltpu.SemaphoreType.DMA
         out = pl.pallas_call(
             functools.partial(kernel, zs, ys),
-            out_shape=jax.ShapeDtypeStruct((rows, width), jnp.bfloat16),
+            out_shape=pltpu.VMEM((rows, width), jnp.bfloat16),
             in_specs=[hbm, hbm, hbm, hbm, smem, smem],
-            out_specs=hbm,
+            out_specs=pl.BlockSpec(memory_space=pl.ANY),
             scratch_shapes=[
                 pltpu.VMEM((blocks, 2, BLOCK, HD), jnp.bfloat16),
                 pltpu.VMEM((blocks, 2, BLOCK, HD), jnp.bfloat16),
                 pltpu.VMEM((rows, width), jnp.bfloat16),
                 pltpu.VMEM((rows, width), jnp.bfloat16),
                 pltpu.VMEM((rows, width), jnp.bfloat16),
-                pltpu.VMEM((2, SLOTS * BLOCK, HD), jnp.bfloat16),
-                pltpu.VMEM((2, SLOTS * BLOCK, HD), jnp.bfloat16),
-                pltpu.VMEM((SIDES, CHUNKS, BLOCK, 2 * HD), jnp.bfloat16),
+                pltpu.VMEM((SLOTS * BLOCK, HD), jnp.bfloat16),
+                pltpu.VMEM((SLOTS * BLOCK, 2 * HD), jnp.bfloat16),
+                pltpu.VMEM((CHUNKS, SIDES, BLOCK, 2 * HD), jnp.bfloat16),
                 pltpu.SMEM((2, SLOTS), jnp.int32),
                 pltpu.SMEM((2, SLOTS), jnp.int32),
                 dma((6,)),

time: 62.6 us -> 53.2 us (0.85)
  Pallas kernels: 60.1 us -> 52.1 us
  local copies, waits for them, and re-layouts: 2.3 us -> 0.97 us
    pallas_call x1, Pallas kernels: 60.1 us -> 52.1 us  [body(): pl.pallas_call(functools.partial(kernel, zs, ys), out_shape=pltpu.VMEM((r...]
    unnamed x1, local copies, waits for them, and re-layouts: 2.3 us -> 0.97 us
where the time goes in v2:
time: 53.2 us; the launch traced here: 53.1 us
  Pallas kernels  52.1 us (98%)
  local copies, waits for them, and re-layouts  0.97 us (2%)
    pallas_call x1, Pallas kernels, body(): pl.pallas_call(functools.partial(kernel, zs, ys), out_shape=pltpu.VMEM((r...  52.1 us

profile of v2, /device:TPU:1, one launch (start us, length us, event | category | flops | bytes accessed | tf_op | source)
XLA Modules:
  0.0 53.1 jit_solution(9224165337477747881)
XLA Ops:
  0.0 52.1 %shard_map.64 = bf16[256,2048]{1,0:T(8,128)(2,1)S(1)} custom-call(bf16[256,2048]{1,0:T(8,128)(2,1)} %bitcast.7, bf16[2,128,256]{2,1,0:T(8,128)(2,1)} %bitcast.9, bf16[2,128,256]{2,1,0:T(8,128)(2,1)} %bitcast.10, bf16[256,2048]{1,0:T(8,128)(2,1)} %bitcast.8, s32[3,1,16]{2,1,0:T(1,128)} %bitcast.11, s32[1,16]{1,0:T(1,128)} %order_ref.1), custom_call_target="tpu_custom_call" | custom-call | tf_op jit(solution)/shard_map/pallas_call | solution.py:376
  52.1 1.0 %copy.8 = bf16[1,256,2048]{2,1,0:T(8,128)(2,1)} copy(bf16[1,256,2048]{2,1,0:T(8,128)(2,1)S(1)} %bitcast.6) | data formatting | bytes 2097152

commit v3 on v2

--- a/solution.py
+++ b/solution.py
@@ -15,7 +15,7 @@
 MASKED = -1e30
 CHUNKS = 8
 HEADS = 4
-SIDES = 2
+SIDES = 4
 LEFT0, LEFT1, RIGHT1, RIGHT0, SIB, OPP0, OPP1, SIB_LEFT, SIB_RIGHT, SIB_OPP0, SIB_OPP1 = range(11)
 PIECES = 11
 HIGH, LOW = 5, 2
@@ -31,30 +31,32 @@
 
 def paths_of_units():
     down, up = turn(1), turn(-1)
-    pairs = [
-        (back(1), down), (back(-1), up), (back(1), down), (back(-1), up),
-        (back(1), down), (back(-1), up), (down, up), (down, up),
-    ]
-    return {(c, d): pairs[c][d] for c in range(CHUNKS) for d in range(SIDES)}
+    plus, minus = back(1), back(-1)
+    both, short = (plus, down, minus, up), (down, up, down, up)
+    halves = [[both] * 6 + [short] * 2] * 2
+    return [{(c, d): pairs[c][d] for c in range(CHUNKS) for d in range(SIDES)} for pairs in halves]
 
 
 PATHS = paths_of_units()
+HELD = {(7, d): ((6, d),) for d in range(SIDES)}
+WAITED = {unit for units in HELD.values() for unit in units}
 EARLY = {HIGH: 4}
 
 
 def hands_on(plane):
-    return [
-        (c, d, path[i], path[i + 1], i + 2 == len(path))
-        for (c, d), path in PATHS.items()
-        for i in range(len(path) - 1)
-        if path[i][1] == plane
-    ]
+    moves = {}
+    for half, paths in enumerate(PATHS):
+        for (c, d), path in paths.items():
+            for i in range(len(path) - 1):
+                if path[i][1] == plane:
+                    moves.setdefault((c, d, path[i], path[i + 1], i + 2 == len(path)), []).append(half)
+    return [(tuple(halves), *move) for move, halves in sorted(moves.items())]
 
 
 def legs(plane, last):
-    out = [(there[0] - here[0], there[1]) for _, _, here, there, _ in hands_on(plane)]
+    out = [(there[0] - here[0], there[1]) for _, _, _, here, there, _ in hands_on(plane)]
     if plane == last:
-        out += [path[0] for path in PATHS.values()]
+        out += [path[0] for paths in PATHS for path in paths.values()]
     return sorted(set(out))
 
 def kernel(
@@ -175,11 +177,13 @@
         await_piece(h, RIGHT1)
         send(h, OPP1).start()
 
-    def send_sib(h):
+    def send_near(h):
         await_piece(h, LEFT1)
         send(h, SIB_LEFT).start()
         await_piece(h, RIGHT0)
         send(h, SIB_RIGHT).start()
+
+    def send_opp(h):
         await_piece(h, OPP0)
         send(h, SIB_OPP0).start()
         await_piece(h, OPP1)
@@ -214,7 +218,8 @@
 
     send_far(0)
     send_own(1)
-    send_sib(0)
+    send_near(0)
+    send_opp(0)
     q_load.wait()
     arrive(0)
     r_load.wait()
@@ -234,8 +239,8 @@
 
     def where_out(c, d):
         h, b, half = c // 4, (c // 2) % 2, c % 2
-        cols = (h * 2 + half) * (HEADS * HD) + d * (HEADS * HD // 2)
-        return pl.ds(pl.multiple_of(b * BLOCK, BLOCK), BLOCK), pl.ds(pl.multiple_of(cols, 2 * HD), 2 * HD)
+        cols = (h * 2 + half) * (HEADS * HD) + d * HD
+        return pl.ds(pl.multiple_of(b * BLOCK, BLOCK), BLOCK), pl.ds(pl.multiple_of(cols, HD), HD)
 
     def to_next(c, d):
         rows, cols = where_out(c, d)
@@ -251,11 +256,17 @@
             device_id=dev_yz(y + step, plane), device_id_type=MESH,
         )
 
-    def first_leg(c, d):
-        path, (rows, cols) = PATHS[c, d], where_out(c, d)
-        if len(path) == 1:
-            return unit(c, d, o_v.at[rows, cols], out_ref.at[rows, cols], out_send, out_recv, *path[0])
-        return unit(c, d, o_v.at[rows, cols], relay.at[c, d], out_send, mid_recv, *path[0])
+    def first_leg(half, c, d):
+        step, plane = PATHS[half][c, d][0]
+        rows, cols = where_out(c, d)
+        return unit(c, d, o_v.at[rows, cols], relay.at[c, d], out_send, mid_recv, step, plane)
+
+    def start_units(units):
+        for half in range(2):
+            @pl.when(y // tps == half)
+            def _(half=half):
+                for c, d in units:
+                    first_leg(half, c, d).start()
 
     def next_leg(c, d, here, there, ends):
         step, plane, (rows, cols) = there[0] - here[0], there[1], where_out(c, d)
@@ -263,9 +274,19 @@
             return unit(c, d, relay.at[c, d], out_ref.at[rows, cols], mid_send, out_recv, step, plane)
         return unit(c, d, relay.at[c, d], relay.at[c, d], mid_send, mid_recv, step, plane)
 
-    def hand_on(c, d, here, there, ends):
-        unit(c, d, relay.at[c, d], relay.at[c, d], mid_send, mid_recv, 0, 0).wait_recv()
-        next_leg(c, d, here, there, ends).start()
+    def from_halves(halves, here):
+        return True if len(halves) == 2 else (y - here[0] + ys) % ys // tps == halves[0]
+
+    def hand_on(halves, c, d, here, there, ends):
+        @pl.when(from_halves(halves, here))
+        def _():
+            unit(c, d, relay.at[c, d], relay.at[c, d], mid_send, mid_recv, 0, 0).wait_recv()
+            next_leg(c, d, here, there, ends).start()
+
+    def handed_on(halves, c, d, here, there, ends):
+        @pl.when(from_halves(halves, here))
+        def _():
+            next_leg(c, d, here, there, ends).wait_send()
 
     def chunk(c, carry):
         h, b, half = c // 4, (c // 2) % 2, c % 2
@@ -276,7 +297,11 @@
 
         @pl.when(c == 2)
         def _():
-            send_sib(1)
+            send_near(1)
+
+        @pl.when(c == 4)
+        def _():
+            send_opp(1)
 
         @pl.when(c == 4)
         def _():
@@ -321,13 +346,12 @@
         for k in range(CHUNKS):
             @pl.when(last & (c == k))
             def _(k=k):
-                for d in range(SIDES):
-                    first_leg(k, d).start()
+                start_units([(k, d) for d in range(SIDES) if (k, d) not in HELD])
 
         for plane, lag in EARLY.items():
             for move in hands_on(plane):
-                if move[0] + lag < CHUNKS:
-                    @pl.when((z == plane) & (c == move[0] + lag))
+                if move[1] + lag < CHUNKS:
+                    @pl.when((z == plane) & (c == move[1] + lag))
                     def _(move=move):
                         hand_on(*move)
 
@@ -335,28 +359,38 @@
 
     lax.fori_loop(0, CHUNKS, chunk, 0)
 
+    @pl.when(last)
+    def _():
+        for held, units in HELD.items():
+            for before in units:
+                first_leg(0, *before).wait_send()
+            start_units([held])
+
     for plane in range(zs):
-        moves = [m for m in hands_on(plane) if plane not in EARLY or m[0] + EARLY[plane] >= CHUNKS]
+        moves = [m for m in hands_on(plane) if plane not in EARLY or m[1] + EARLY[plane] >= CHUNKS]
         if moves:
             @pl.when(z == plane)
             def _(moves=moves):
                 for move in moves:
                     hand_on(*move)
 
-    def finish(c, carry):
+    for c in range(CHUNKS):
         for d in range(SIDES):
             to_next(c, d).wait_recv()
+            if (c, d) not in WAITED:
+                to_next(c, d).wait_send()
+
+    @pl.when(~last)
+    def _():
+        for c, d in sorted(WAITED):
             to_next(c, d).wait_send()
-        return carry
-
-    lax.fori_loop(0, CHUNKS, finish, 0)
 
     for plane in range(zs):
         if hands_on(plane):
             @pl.when(z == plane)
             def _(plane=plane):
                 for move in hands_on(plane):
-                    next_leg(*move).wait_send()
+                    handed_on(*move)
 
     for h in range(2):
         for tag in range(PIECES):
@@ -386,7 +420,7 @@
                 pltpu.VMEM((rows, width), jnp.bfloat16),
                 pltpu.VMEM((SLOTS * BLOCK, HD), jnp.bfloat16),
                 pltpu.VMEM((SLOTS * BLOCK, 2 * HD), jnp.bfloat16),
-                pltpu.VMEM((CHUNKS, SIDES, BLOCK, 2 * HD), jnp.bfloat16),
+                pltpu.VMEM((CHUNKS, SIDES, BLOCK, HD), jnp.bfloat16),
                 pltpu.SMEM((2, SLOTS), jnp.int32),
                 pltpu.SMEM((2, SLOTS), jnp.int32),
                 dma((6,)),

time: 53.2 us -> 51.3 us (0.964)
  Pallas kernels: 52.1 us -> 50.1 us
    pallas_call x1, Pallas kernels: 52.1 us -> 50.1 us  [body(): pl.pallas_call(functools.partial(kernel, zs, ys), out_shape=pltpu.VMEM((r...]
where the time goes in v3:
time: 51.3 us; the launch traced here: 51.1 us
  Pallas kernels  50.1 us (98%)
  local copies, waits for them, and re-layouts  0.97 us (2%)
    pallas_call x1, Pallas kernels, body(): pl.pallas_call(functools.partial(kernel, zs, ys), out_shape=pltpu.VMEM((r...  50.1 us

profile of v3, /device:TPU:1, one launch (start us, length us, event | category | flops | bytes accessed | tf_op | source)
XLA Modules:
  0.0 51.1 jit_solution(9553653497879871111)
XLA Ops:
  0.0 50.1 %shard_map.64 = bf16[256,2048]{1,0:T(8,128)(2,1)S(1)} custom-call(bf16[256,2048]{1,0:T(8,128)(2,1)} %bitcast.7, bf16[2,128,256]{2,1,0:T(8,128)(2,1)} %bitcast.9, bf16[2,128,256]{2,1,0:T(8,128)(2,1)} %bitcast.10, bf16[256,2048]{1,0:T(8,128)(2,1)} %bitcast.8, s32[3,1,16]{2,1,0:T(1,128)} %bitcast.11, s32[1,16]{1,0:T(1,128)} %order_ref.1), custom_call_target="tpu_custom_call" | custom-call | tf_op jit(solution)/shard_map/pallas_call | solution.py:410
  50.2 1.0 %copy.8 = bf16[1,256,2048]{2,1,0:T(8,128)(2,1)} copy(bf16[1,256,2048]{2,1,0:T(8,128)(2,1)S(1)} %bitcast.6) | data formatting | bytes 2097152

commit v4 on v3

--- a/solution.py
+++ b/solution.py
@@ -40,7 +40,7 @@
 PATHS = paths_of_units()
 HELD = {(7, d): ((6, d),) for d in range(SIDES)}
 WAITED = {unit for units in HELD.values() for unit in units}
-EARLY = {HIGH: 4}
+EARLY = {HIGH: 3}
 
 
 def hands_on(plane):

time: 51.3 us -> 49.5 us (0.965)
  Pallas kernels: 50.1 us -> 48.3 us
    pallas_call x1, Pallas kernels: 50.1 us -> 48.3 us  [body(): pl.pallas_call(functools.partial(kernel, zs, ys), out_shape=pltpu.VMEM((r...]
where the time goes in v4:
time: 49.5 us; the launch traced here: 49.3 us
  Pallas kernels  48.3 us (98%)
  local copies, waits for them, and re-layouts  0.97 us (2%)
    pallas_call x1, Pallas kernels, body(): pl.pallas_call(functools.partial(kernel, zs, ys), out_shape=pltpu.VMEM((r...  48.3 us

profile of v4, /device:TPU:1, one launch (start us, length us, event | category | flops | bytes accessed | tf_op | source)
XLA Modules:
  0.0 49.3 jit_solution(13672596484963471118)
XLA Ops:
  0.0 48.3 %shard_map.64 = bf16[256,2048]{1,0:T(8,128)(2,1)S(1)} custom-call(bf16[256,2048]{1,0:T(8,128)(2,1)} %bitcast.7, bf16[2,128,256]{2,1,0:T(8,128)(2,1)} %bitcast.9, bf16[2,128,256]{2,1,0:T(8,128)(2,1)} %bitcast.10, bf16[256,2048]{1,0:T(8,128)(2,1)} %bitcast.8, s32[3,1,16]{2,1,0:T(1,128)} %bitcast.11, s32[1,16]{1,0:T(1,128)} %order_ref.1), custom_call_target="tpu_custom_call" | custom-call | tf_op jit(solution)/shard_map/pallas_call | solution.py:410
  48.3 1.0 %copy.8 = bf16[1,256,2048]{2,1,0:T(8,128)(2,1)} copy(bf16[1,256,2048]{2,1,0:T(8,128)(2,1)S(1)} %bitcast.6) | data formatting | bytes 2097152

commit v5 on v4

--- a/solution.py
+++ b/solution.py
@@ -167,8 +167,8 @@
     def await_piece(h, tag):
         piece(h, tag, *received[tag]).wait_recv()
 
-    def send_own(h):
-        for tag in (LEFT0, RIGHT1, LEFT1, RIGHT0, SIB):
+    def send_own(h, tags=(LEFT0, RIGHT1, LEFT1, RIGHT0, SIB)):
+        for tag in tags:
             send(h, tag).start()
 
     def send_far(h):
@@ -217,8 +217,9 @@
             slot_ok[b, s] = jnp.where(valid[s], 1, 0)
 
     send_far(0)
-    send_own(1)
+    send_own(1, (LEFT0, RIGHT1))
     send_near(0)
+    send_own(1, (LEFT1, RIGHT0, SIB))
     send_opp(0)
     q_load.wait()
     arrive(0)
@@ -374,9 +375,12 @@
                 for move in moves:
                     hand_on(*move)
 
+    for h in range(2):
+        for tag in range(PIECES):
+            send(h, tag).wait_send()
+
     for c in range(CHUNKS):
         for d in range(SIDES):
-            to_next(c, d).wait_recv()
             if (c, d) not in WAITED:
                 to_next(c, d).wait_send()
 
@@ -392,9 +396,9 @@
                 for move in hands_on(plane):
                     handed_on(*move)
 
-    for h in range(2):
-        for tag in range(PIECES):
-            send(h, tag).wait_send()
+    for c in range(CHUNKS):
+        for d in range(SIDES):
+            to_next(c, d).wait_recv()
 
 
 def solution(mesh):

time: 49.5 us -> 49.3 us (level)
  no operation moved by 1% of the time
where the time goes in v5:
time: 49.3 us; the launch traced here: 49.1 us
  Pallas kernels  48.1 us (98%)
  local copies, waits for them, and re-layouts  0.97 us (2%)
    pallas_call x1, Pallas kernels, body(): pl.pallas_call(functools.partial(kernel, zs, ys), out_shape=pltpu.VMEM((r...  48.1 us

profile of v5, /device:TPU:1, one launch (start us, length us, event | category | flops | bytes accessed | tf_op | source)
XLA Modules:
  0.0 49.1 jit_solution(17954462073411472963)
XLA Ops:
  0.0 48.1 %shard_map.64 = bf16[256,2048]{1,0:T(8,128)(2,1)S(1)} custom-call(bf16[256,2048]{1,0:T(8,128)(2,1)} %bitcast.7, bf16[2,128,256]{2,1,0:T(8,128)(2,1)} %bitcast.9, bf16[2,128,256]{2,1,0:T(8,128)(2,1)} %bitcast.10, bf16[256,2048]{1,0:T(8,128)(2,1)} %bitcast.8, s32[3,1,16]{2,1,0:T(1,128)} %bitcast.11, s32[1,16]{1,0:T(1,128)} %order_ref.1), custom_call_target="tpu_custom_call" | custom-call | tf_op jit(solution)/shard_map/pallas_call | solution.py:414
  48.2 1.0 %copy.8 = bf16[1,256,2048]{2,1,0:T(8,128)(2,1)} copy(bf16[1,256,2048]{2,1,0:T(8,128)(2,1)S(1)} %bitcast.6) | data formatting | bytes 2097152

commit v6 on v5

--- a/solution.py
+++ b/solution.py
@@ -248,7 +248,7 @@
         return pltpu.make_async_remote_copy(
             src_ref=o_v.at[rows, cols], dst_ref=out_ref.at[rows, cols],
             send_sem=out_send.at[c, d], recv_sem=out_recv.at[c, d],
-            device_id=(section + 1, ctx, tp), device_id_type=MESH,
+            device_id=((section + 1) % lax.axis_size("section"), ctx, tp), device_id_type=MESH,
         )
 
     def unit(c, d, src, dst, send_sem, recv_sem, step, plane):

time: 49.3 us -> 49.1 us (level)
  no operation moved by 1% of the time
where the time goes in v6:
time: 49.1 us; the launch traced here: 48.9 us
  Pallas kernels  47.9 us (98%)
  local copies, waits for them, and re-layouts  0.97 us (2%)
    pallas_call x1, Pallas kernels, body(): pl.pallas_call(functools.partial(kernel, zs, ys), out_shape=pltpu.VMEM((r...  47.9 us

profile of v6, /device:TPU:1, one launch (start us, length us, event | category | flops | bytes accessed | tf_op | source)
XLA Modules:
  0.0 48.9 jit_solution(1674504221177615793)
XLA Ops:
  0.0 47.9 %shard_map.64 = bf16[256,2048]{1,0:T(8,128)(2,1)S(1)} custom-call(bf16[256,2048]{1,0:T(8,128)(2,1)} %bitcast.7, bf16[2,128,256]{2,1,0:T(8,128)(2,1)} %bitcast.9, bf16[2,128,256]{2,1,0:T(8,128)(2,1)} %bitcast.10, bf16[256,2048]{1,0:T(8,128)(2,1)} %bitcast.8, s32[3,1,16]{2,1,0:T(1,128)} %bitcast.11, s32[1,16]{1,0:T(1,128)} %order_ref.1), custom_call_target="tpu_custom_call" | custom-call | tf_op jit(solution)/shard_map/pallas_call | solution.py:414
  47.9 1.0 %copy.8 = bf16[1,256,2048]{2,1,0:T(8,128)(2,1)} copy(bf16[1,256,2048]{2,1,0:T(8,128)(2,1)S(1)} %bitcast.6) | data formatting | bytes 2097152
